TPU v7x, 32 devices: a whole 2x2x4 slice. The times are simulated.
32 devices in a mesh: half: 2 (over core), cls: 16 (over z, y, x).
Axes of the slice: x: 2, y: 2, z: 4, core: 2. Of those that a mesh axis runs over, the one named last changes fastest.
Arguments:
- particles: bfloat16 [2, 1024, 128, 128], P('half', 'cls'), may hold values from -6 to 6
- assign: int32 [2, 1024], P('half', 'cls'), may hold values from 0 to 15, as said below
- rotation: int32 [2, 1024], P('half', 'cls'), may hold values from 0 to 35
- group: int32 [2, 1024], P('half', 'cls'), may hold values from 0 to 255
- ctf: float32 [256, 64], replicated, may hold values from -1 to 1
Outputs:
- class_avg: bfloat16 [2, 16, 128, 128], P('half', 'cls')
- residual: bfloat16 [2, 1024, 128, 128], P('half', 'cls')
- scores: bfloat16 [2, 1024, 36], P('half', 'cls')
- leverage: bfloat16 [2, 1024], P('half', 'cls')
Inputs may be any that keep to these rules, and one draw needn't show every extreme that they name: `assign`: among the 64 particles of one device no class appears more than 8 times, and one class appears exactly 8 times among every device's particles.
All inputs are finite; a program needn't handle non-finite values.
Results may differ from a plain program's by a relative error of at most 0.0065.
Values may be sent and summed in bfloat16 or wider, within the bound.
A program may use at most 128 MiB of HBM per device.

v0:
```python
import functools
import math

import jax
import jax.numpy as jnp
from jax import lax
from jax.experimental import pallas as pl
from jax.experimental.pallas import tpu as pltpu
from jax.sharding import PartitionSpec as P

NROT = 36
TAU = 1.0
STEP = 8
QUAD = 4
MESH = pl.DeviceIdType.MESH
HIGHEST = lax.Precision.HIGHEST
VMEM_BYTES = 24 * 1024 * 1024
WIDE_BYTES = 62 * 1024 * 1024


def vmem():
    return pl.BlockSpec(memory_space=pltpu.VMEM)


def smem():
    return pl.BlockSpec(memory_space=pltpu.SMEM)


def mix(turn, angles):
    scaled = turn * angles
    offset = scaled // NROT
    fraction = (scaled - offset * NROT).astype(jnp.float32) / NROT
    first = (1.0 - fraction).astype(jnp.bfloat16).astype(jnp.float32)
    second = fraction.astype(jnp.bfloat16).astype(jnp.float32)
    return offset, first, second


def align(image, turn):
    angles = image.shape[1]
    offset, first, second = mix(turn, angles)
    rolled = pltpu.roll(image, offset, 1)
    return first * rolled + second * pltpu.roll(rolled, 1, 1)


def one_hot(row, size):
    places = lax.broadcasted_iota(jnp.int32, (size, row.shape[1]), 0)
    return (places == row).astype(jnp.float32)


def columns_of(ctf, groups):
    return lax.dot_general(
        ctf,
        one_hot(groups, ctf.shape[1]),
        (((1,), (0,)), ((), ())),
        precision=HIGHEST,
        preferred_element_type=jnp.float32,
    )


def fill_columns(columns_ref, ctf_ref, group_ref):
    columns_ref[...] = jnp.zeros_like(columns_ref)
    columns_ref[:, : group_ref.shape[1]] = columns_of(ctf_ref[...], group_ref[...])


def step_columns(columns_ref, step):
    lanes = columns_ref.shape[1]
    return pltpu.roll(columns_ref[...], lax.rem(lanes - step * STEP, lanes), 1)


def stacked(columns, place, lanes):
    column = columns[:, place : place + 1]
    wide = jnp.broadcast_to(column, (columns.shape[0], lanes))
    return jnp.concatenate([wide, wide], axis=0)


def sums_kernel(assign_ref, turn_ref, group_ref, ctf_ref, images_ref, out_ref, total, columns_ref):
    step = pl.program_id(0)

    @pl.when(step == 0)
    def _():
        total[...] = jnp.zeros_like(total)
        fill_columns(columns_ref, ctf_ref, group_ref)

    columns = step_columns(columns_ref, step)
    for place in range(STEP):
        particle = step * STEP + place
        image = images_ref[place].astype(jnp.float32)
        weight = stacked(columns, place, image.shape[1])
        owner = assign_ref[0, particle]
        total[owner] += weight * align(image, turn_ref[0, particle])

    @pl.when(step == pl.num_programs(0) - 1)
    def _():
        out_ref[...] = total[...].astype(jnp.bfloat16)


def share_kernel(
    count,
    sums_ref,
    assign_ref,
    group_ref,
    ctf_ref,
    average_ref,
    lever_ref,
    partner_ref,
    own_code,
    codes,
    landed,
    staged,
    gathered,
    average,
    code_send,
    code_recv,
    quad_send,
    quad_recv,
    far_send,
    far_recv,
    avg_send,
    pass_send,
    avg_recv,
):
    half = lax.axis_index("half")
    me = lax.axis_index("cls")
    other = 1 - half
    layers = count // QUAD
    layer = me // QUAD
    spot = me % QUAD
    particles = assign_ref.shape[1]

    barrier = pltpu.get_barrier_semaphore()

    def greet(k, _):
        peer = lax.rem(me + k, count)
        pl.semaphore_signal(barrier, inc=1, device_id=(half, peer), device_id_type=MESH)
        return 0

    def greet_other(k, _):
        peer = lax.rem(layer + k, layers) * QUAD + spot
        pl.semaphore_signal(barrier, inc=1, device_id=(other, peer), device_id_type=MESH)
        return 0

    lax.fori_loop(1, count, greet, 0)
    lax.fori_loop(0, layers, greet_other, 0)
    own_code[0] = jnp.concatenate([assign_ref[...], group_ref[...]], axis=1).astype(jnp.float32)
    pl.semaphore_wait(barrier, count - 1 + layers)

    def code_copy(source, peer):
        return pltpu.make_async_remote_copy(
            src_ref=own_code.at[0],
            dst_ref=codes.at[source],
            send_sem=code_send.at[peer],
            recv_sem=code_recv.at[source],
            device_id=(half, peer),
            device_id_type=MESH,
        )

    def quad_copy(level, source, target):
        return pltpu.make_async_remote_copy(
            src_ref=sums_ref.at[level * QUAD + target],
            dst_ref=landed.at[level * QUAD + source],
            send_sem=quad_send.at[level * QUAD + target],
            recv_sem=quad_recv.at[level * QUAD + source],
            device_id=(half, layer * QUAD + target),
            device_id_type=MESH,
        )

    def far_copy(source, target):
        return pltpu.make_async_remote_copy(
            src_ref=staged.at[target],
            dst_ref=gathered.at[source],
            send_sem=far_send.at[target],
            recv_sem=far_recv.at[source],
            device_id=(half, target * QUAD + spot),
            device_id_type=MESH,
        )

    def avg_copy(source, target):
        return pltpu.make_async_remote_copy(
            src_ref=average,
            dst_ref=partner_ref.at[source * QUAD + spot],
            send_sem=avg_send.at[target],
            recv_sem=avg_recv.at[source * QUAD + spot],
            device_id=(other, target * QUAD + spot),
            device_id_type=MESH,
        )

    def pass_copy(level, source, target):
        return pltpu.make_async_remote_copy(
            src_ref=partner_ref.at[level * QUAD + source],
            dst_ref=partner_ref.at[level * QUAD + source],
            send_sem=pass_send.at[level * QUAD + target],
            recv_sem=avg_recv.at[level * QUAD + source],
            device_id=(half, layer * QUAD + target),
            device_id_type=MESH,
        )

    def send_code(k, _):
        code_copy(me, lax.rem(me + k, count)).start()
        return 0

    def send_quad(k, _):
        level = lax.rem(layer + k, layers)
        for j in range(1, QUAD):
            quad_copy(level, spot, lax.rem(spot + j, QUAD)).start()
        return 0

    lax.fori_loop(1, layers + 1, send_quad, 0)
    lax.fori_loop(1, count, send_code, 0)

    def quad_sum(level):
        total = sums_ref[level * QUAD + spot].astype(jnp.float32)
        for j in range(1, QUAD):
            source = lax.rem(spot + j, QUAD)
            quad_copy(level, source, source).wait_recv()
            total += landed[level * QUAD + source].astype(jnp.float32)
        return total

    def send_far(k, _):
        level = lax.rem(layer + k, layers)
        staged[level] = quad_sum(level).astype(jnp.bfloat16)
        far_copy(layer, level).start()
        return 0

    lax.fori_loop(1, layers, send_far, 0)

    def tally(code):
        owners = one_hot(code[:, :particles].astype(jnp.int32), count)
        kinds = one_hot(code[:, particles:].astype(jnp.int32), ctf_ref.shape[1])
        return lax.dot_general(
            owners.astype(jnp.bfloat16),
            kinds.astype(jnp.bfloat16),
            (((1,), (1,)), ((), ())),
            preferred_element_type=jnp.float32,
        )

    def add_code(k, counts):
        source = lax.rem(me + count - k, count)
        code_copy(source, source).wait_recv()
        return counts + tally(codes[source])

    counts = lax.fori_loop(1, count, add_code, tally(own_code[0]))
    table = ctf_ref[...]
    den = lax.dot_general(
        table * table,
        counts,
        (((1,), (1,)), ((), ())),
        precision=HIGHEST,
        preferred_element_type=jnp.float32,
    )
    mine = lax.broadcasted_iota(jnp.int32, den.shape, 1) == me
    column = jnp.sum(jnp.where(mine, den, 0.0), axis=1, keepdims=True) + TAU
    denom = jnp.concatenate([column, column], axis=0)

    def add_far(k, total):
        source = lax.rem(layer + count - k, layers)
        far_copy(source, source).wait_recv()
        return total + gathered[source].astype(jnp.float32)

    total = lax.fori_loop(1, layers, add_far, quad_sum(layer))
    average[...] = (total / denom).astype(jnp.bfloat16)

    def send_avg(k, _):
        avg_copy(layer, lax.rem(layer + k, layers)).start()
        return 0

    lax.fori_loop(0, layers, send_avg, 0)
    average_ref[...] = average[...]
    weights = columns_of(table, group_ref[...])
    chosen = jnp.dot(
        den,
        one_hot(assign_ref[...], count),
        precision=HIGHEST,
        preferred_element_type=jnp.float32,
    )
    lever = jnp.sum(weights * weights / (chosen + TAU), axis=0, keepdims=True)
    lever_ref[...] = (lever / table.shape[0]).astype(jnp.bfloat16)

    def pass_on(k, _):
        level = lax.rem(layer + k, layers)
        avg_copy(level, level).wait_recv()
        for j in range(1, QUAD):
            pass_copy(level, spot, lax.rem(spot + j, QUAD)).start()
        return 0

    lax.fori_loop(0, layers, pass_on, 0)

    def finish_code(k, _):
        code_copy(me, lax.rem(me + k, count)).wait_send()
        return 0

    def finish_far(k, _):
        far_copy(layer, lax.rem(layer + k, layers)).wait_send()
        return 0

    def finish_level(k, _):
        level = lax.rem(layer + k, layers)
        avg_copy(layer, level).wait_send()
        for j in range(1, QUAD):
            peer = lax.rem(spot + j, QUAD)
            quad_copy(level, spot, peer).wait_send()
            pass_copy(level, peer, peer).wait_recv()
            pass_copy(level, spot, peer).wait_send()
        return 0

    lax.fori_loop(1, count, finish_code, 0)
    lax.fori_loop(1, layers, finish_far, 0)
    lax.fori_loop(0, layers, finish_level, 0)


def compare_kernel(
    assign_ref,
    turn_ref,
    group_ref,
    ctf_ref,
    partner_ref,
    average_ref,
    lever_ref,
    images_ref,
    residual_ref,
    scores_ref,
    average_out,
    lever_out,
    columns_ref,
    image_power,
    predicted_power,
    folded,
):
    step = pl.program_id(0)

    @pl.when(step == 0)
    def _():
        fill_columns(columns_ref, ctf_ref, group_ref)
        average_out[...] = average_ref[...]
        lever_out[...] = lever_ref[...]

    columns = step_columns(columns_ref, step)
    rows, angles = images_ref.shape[1:]

    def fold(values):
        return jnp.sum(values.reshape(rows // 8, 8, angles), axis=0)

    for place in range(STEP):
        particle = step * STEP + place
        raw_image = images_ref[place]
        image = raw_image.astype(jnp.float32)
        weight = stacked(columns, place, angles)
        owner = assign_ref[0, particle]
        rounded = (weight * partner_ref[owner].astype(jnp.float32)).astype(jnp.bfloat16)
        predicted = rounded.astype(jnp.float32)
        residual_ref[place] = (align(image, turn_ref[0, particle]) - predicted).astype(jnp.bfloat16)
        cross = lax.dot_general(
            raw_image, rounded, (((0,), (0,)), ((), ())), preferred_element_type=jnp.float32
        )
        turned = cross[:8]
        for tile in range(1, angles // 8):
            turned += pltpu.roll(cross[tile * 8 : tile * 8 + 8], angles - tile * 8, 1)
        spot = pl.ds(pl.multiple_of(particle * 8, 8), 8)
        folded[spot, :] = turned
        image_power[spot, :] = fold(image * image)
        predicted_power[spot, :] = fold(predicted * predicted)

    @pl.when(step == pl.num_programs(0) - 1)
    def _():
        number = folded.shape[0] // 8

        def part(ref, k):
            return ref[pl.ds(k, number, stride=8), :]

        corr = part(folded, 0)
        first = part(image_power, 0)
        second = part(predicted_power, 0)
        for k in range(1, 8):
            corr += pltpu.roll(part(folded, k), angles - k, 1)
            first += part(image_power, k)
            second += part(predicted_power, k)
        pixels = rows * angles
        ones = jnp.ones((1, angles), jnp.float32)

        def across(left, right, dims):
            return lax.dot_general(
                left, right, (dims, ((), ())), precision=HIGHEST, preferred_element_type=jnp.float32
            )

        first = jnp.sqrt(across(ones, first, ((1,), (1,))) / pixels + 1e-05)
        second = jnp.sqrt(across(ones, second, ((1,), (1,))) / pixels + 1e-05)
        turns = lax.broadcasted_iota(jnp.int32, (angles, angles), 1)
        shifts = lax.broadcasted_iota(jnp.int32, (angles, angles), 0)
        offset, one, two = mix(turns, angles)
        offset = lax.rem(offset, angles)
        table = jnp.where(shifts == offset, one, 0.0) + jnp.where(
            shifts == lax.rem(offset + 1, angles), two, 0.0
        )
        raw = across(table, corr, ((0,), (1,)))
        scores = raw / (math.sqrt(pixels) * first * second)
        scores_ref[...] = scores[:NROT].astype(jnp.bfloat16)


def body(particles, assign, rotation, group, ctf):
    images = particles[0]
    number, rows, angles = images.shape
    table = ctf.T
    shells = ctf.shape[1]
    count = lax.axis_size("cls")
    layers = count // QUAD
    steps = number // STEP
    params = pltpu.CompilerParams(vmem_limit_bytes=VMEM_BYTES)
    block = pl.BlockSpec((STEP, rows, angles), lambda i: (i, 0, 0))

    sums = pl.pallas_call(
        sums_kernel,
        grid=(steps,),
        out_shape=jax.ShapeDtypeStruct((count, rows, angles), jnp.bfloat16),
        in_specs=[smem(), smem(), vmem(), vmem(), block],
        out_specs=vmem(),
        scratch_shapes=[
            pltpu.VMEM((count, rows, angles), jnp.float32),
            pltpu.VMEM((shells, 128), jnp.float32),
        ],
        compiler_params=pltpu.CompilerParams(vmem_limit_bytes=WIDE_BYTES),
        name="class_sums",
    )(assign, rotation, group, table, images)

    average, lever, partner = pl.pallas_call(
        functools.partial(share_kernel, count),
        out_shape=(
            jax.ShapeDtypeStruct((rows, angles), jnp.bfloat16),
            jax.ShapeDtypeStruct((1, number), jnp.bfloat16),
            jax.ShapeDtypeStruct((count, rows, angles), jnp.bfloat16),
        ),
        in_specs=[vmem(), vmem(), vmem(), vmem()],
        out_specs=(vmem(), vmem(), pl.BlockSpec(memory_space=pl.ANY)),
        scratch_shapes=[
            pltpu.VMEM((1, 1, 2 * number), jnp.float32),
            pltpu.VMEM((count, 1, 2 * number), jnp.float32),
            pltpu.VMEM((count, rows, angles), jnp.bfloat16),
            pltpu.VMEM((layers, rows, angles), jnp.bfloat16),
            pltpu.VMEM((layers, rows, angles), jnp.bfloat16),
            pltpu.VMEM((rows, angles), jnp.bfloat16),
        ]
        + [pltpu.SemaphoreType.DMA((count,))] * 4
        + [pltpu.SemaphoreType.DMA((layers,))] * 3
        + [pltpu.SemaphoreType.DMA((count,))] * 2,
        compiler_params=pltpu.CompilerParams(
            collective_id=0, has_side_effects=True, vmem_limit_bytes=VMEM_BYTES
        ),
        name="share",
    )(sums, assign, group, table)

    residual, scores, average, lever = pl.pallas_call(
        compare_kernel,
        grid=(steps,),
        out_shape=(
            jax.ShapeDtypeStruct((number, rows, angles), jnp.bfloat16),
            jax.ShapeDtypeStruct((NROT, number), jnp.bfloat16),
            jax.ShapeDtypeStruct((rows, angles), jnp.bfloat16),
            jax.ShapeDtypeStruct((1, number), jnp.bfloat16),
        ),
        in_specs=[smem(), smem()] + [vmem()] * 5 + [block],
        out_specs=(block, vmem(), vmem(), vmem()),
        scratch_shapes=[pltpu.VMEM((shells, 128), jnp.float32)]
        + [pltpu.VMEM((number * 8, angles), jnp.float32)] * 3,
        compiler_params=params,
        name="compare",
    )(assign, rotation, group, table, partner, average, lever, images)
    return (average[None, None], residual[None], scores.T[None], lever)


def solution(mesh):
    in_specs = (
        P("half", "cls", None, None),
        P("half", "cls"),
        P("half", "cls"),
        P("half", "cls"),
        P(),
    )
    out_specs = (
        P("half", "cls", None, None),
        P("half", "cls", None, None),
        P("half", "cls", None),
        P("half", "cls"),
    )
    return jax.shard_map(body, mesh=mesh, in_specs=in_specs, out_specs=out_specs, check_vma=False)
```

profile of v0, /device:TPU:0, one launch (start us, length us, event | category | flops | bytes accessed | tf_op | source)
XLA Modules:
  0.0 49.9 jit_solution(12249147776126121150)
XLA Ops:
  0.6 0.0 copy-start.4
  0.6 0.0 copy-start.3
  0.7 0.0 copy-start.5
  0.7 0.0 copy-start.2
  0.7 8.0 %class_sums.1.sums_ref = bf16[16,128,128]{2,1,0:T(8,128)(2,1)} custom-call(s32[1,64]{1,0:T(1,128)} %assign_ref.5, s32[1,64]{1,0:T(1,128)} %turn_ref.3, s32[1,64]{1,0:T(1,128)} %group_ref.5, f32[64,256]{1,0:T(8,128)} %bitcast.9, bf16[64,128,128]{2,1,0:T(8,128)(2,1)} %bitcast.7), custom_call_target="tpu_custom_call" | custom-call | tf_op jit(solution)/shard_map/class_sums/pallas_call | solution.py:409
  8.7 0.0 copy-done.4
  8.7 0.0 copy-done.3
  8.7 0.0 copy-done.2
  8.7 0.0 copy-start.1
  8.7 1.0 %copy-done.1 = bf16[16,128,128]{2,1,0:T(8,128)(2,1)S(1)} copy-done((bf16[16,128,128]{2,1,0:T(8,128)(2,1)S(1)}, bf16[16,128,128]{2,1,0:T(8,128)(2,1)}, u32[]{:S(2)}) %copy-start.1) | copy-done | bytes 524312
  9.7 27.0 %share.1 = (bf16[128,128]{1,0:T(8,128)(2,1)S(1)}, bf16[1,64]{1,0:T(2,128)(2,1)S(1)}, bf16[16,128,128]{2,1,0:T(8,128)(2,1)S(1)}) custom-call(bf16[16,128,128]{2,1,0:T(8,128)(2,1)S(1)} %copy-done.1, s32[1,64]{1,0:T(1,128)S(1)} %copy-done.3, s32[1,64]{1,0:T(1,128)S(1)} %copy-done.4, f32[64,256]{1,0:T(8,128)S(1)} %bitcast.10), custom_call_target="tpu_custom_call" | custom-call | tf_op jit(solution)/shard_map/share/pallas_call | solution.py:423
  36.8 0.0 copy-done.5
  36.8 0.0 copy-start
  36.8 1.6 %copy-done = bf16[1,64,128,128]{3,2,1,0:T(8,128)(2,1)S(1)} copy-done((bf16[1,64,128,128]{3,2,1,0:T(8,128)(2,1)S(1)}, bf16[1,64,128,128]{3,2,1,0:T(8,128)(2,1)}, u32[]{:S(2)}) %copy-start) | copy-done | bytes 2097176
  38.4 11.5 %compare.1 = (bf16[64,128,128]{2,1,0:T(8,128)(2,1)}, bf16[36,64]{1,0:T(8,128)(2,1)}, bf16[128,128]{1,0:T(8,128)(2,1)}, bf16[1,64]{1,0:T(2,128)(2,1)}) custom-call(s32[1,64]{1,0:T(1,128)S(1)} %copy-done.3, s32[1,64]{1,0:T(1,128)S(1)} %copy-done.5, s32[1,64]{1,0:T(1,128)S(1)} %copy-done.4, f32[64,256]{1,0:T(8,128)S(1)} %bitcast.11, ...), custom_call_target="tpu_custom_call" | custom-call | tf_op jit(solution)/shard_map/compare/pallas_call | solution.py:449
Async XLA Ops:
  0.6 8.1 %copy-start.4 = (s32[1,64]{1,0:T(1,128)S(1)}, s32[1,64]{1,0:T(1,128)}, u32[]{:S(2)}) copy-start(s32[1,64]{1,0:T(1,128)} %group_ref.5) | copy-start | bytes 772
  0.6 8.0 %copy-start.3 = (s32[1,64]{1,0:T(1,128)S(1)}, s32[1,64]{1,0:T(1,128)}, u32[]{:S(2)}) copy-start(s32[1,64]{1,0:T(1,128)} %assign_ref.5) | copy-start | bytes 772
  0.7 36.1 %copy-start.5 = (s32[1,64]{1,0:T(1,128)S(1)}, s32[1,64]{1,0:T(1,128)}, u32[]{:S(2)}) copy-start(s32[1,64]{1,0:T(1,128)} %turn_ref.3) | copy-start | bytes 772
  0.7 8.0 %copy-start.2 = (f32[256,64]{0,1:T(8,128)S(1)}, f32[256,64]{0,1:T(8,128)}, u32[]{:S(2)}) copy-start(f32[256,64]{0,1:T(8,128)} %param.9) | copy-start | bytes 196612
  8.7 1.0 %copy-start.1 = (bf16[16,128,128]{2,1,0:T(8,128)(2,1)S(1)}, bf16[16,128,128]{2,1,0:T(8,128)(2,1)}, u32[]{:S(2)}) copy-start(bf16[16,128,128]{2,1,0:T(8,128)(2,1)} %class_sums.1.sums_ref) | copy-start | bytes 1572868
  36.8 1.6 %copy-start = (bf16[1,64,128,128]{3,2,1,0:T(8,128)(2,1)S(1)}, bf16[1,64,128,128]{3,2,1,0:T(8,128)(2,1)}, u32[]{:S(2)}) copy-start(bf16[1,64,128,128]{3,2,1,0:T(8,128)(2,1)} %param.5) | copy-start | bytes 6291460
where the time goes:
time: 50.2 us; the launch traced here: 49.9 us
  Pallas kernels  46.5 us (93%)
  local copies, waits for them, and re-layouts  2.64 us (5%)
  between operations  0.71 us (1%)
    pallas_call x1, Pallas kernels, body(): pl.pallas_call(functools.partial(share_kernel, count), out_shape=(jax.Sha...  27 us
    pallas_call x1, Pallas kernels, body(): pl.pallas_call(compare_kernel, grid=(steps,), out_shape=(jax.ShapeDtypeSt...  11.5 us
    pallas_call x1, Pallas kernels, body(): pl.pallas_call(sums_kernel, grid=(steps,), out_shape=jax.ShapeDtypeStruct...  8.01 us
    unnamed x12, local copies, waits for them, and re-layouts  2.64 us

commit v1 on v0

--- a/solution.py
+++ b/solution.py
@@ -14,7 +14,6 @@
 QUAD = 4
 MESH = pl.DeviceIdType.MESH
 HIGHEST = lax.Precision.HIGHEST
-VMEM_BYTES = 24 * 1024 * 1024
 WIDE_BYTES = 62 * 1024 * 1024
 
 
@@ -22,8 +21,8 @@
     return pl.BlockSpec(memory_space=pltpu.VMEM)
 
 
-def smem():
-    return pl.BlockSpec(memory_space=pltpu.SMEM)
+def anywhere():
+    return pl.BlockSpec(memory_space=pl.ANY)
 
 
 def mix(turn, angles):
@@ -39,7 +38,9 @@
     angles = image.shape[1]
     offset, first, second = mix(turn, angles)
     rolled = pltpu.roll(image, offset, 1)
-    return first * rolled + second * pltpu.roll(rolled, 1, 1)
+    return first * rolled.astype(jnp.float32) + second * pltpu.roll(rolled, 1, 1).astype(
+        jnp.float32
+    )
 
 
 def one_hot(row, size):
@@ -73,42 +74,34 @@
     return jnp.concatenate([wide, wide], axis=0)
 
 
-def sums_kernel(assign_ref, turn_ref, group_ref, ctf_ref, images_ref, out_ref, total, columns_ref):
-    step = pl.program_id(0)
-
-    @pl.when(step == 0)
-    def _():
-        total[...] = jnp.zeros_like(total)
-        fill_columns(columns_ref, ctf_ref, group_ref)
-
-    columns = step_columns(columns_ref, step)
-    for place in range(STEP):
-        particle = step * STEP + place
-        image = images_ref[place].astype(jnp.float32)
-        weight = stacked(columns, place, image.shape[1])
-        owner = assign_ref[0, particle]
-        total[owner] += weight * align(image, turn_ref[0, particle])
-
-    @pl.when(step == pl.num_programs(0) - 1)
-    def _():
-        out_ref[...] = total[...].astype(jnp.bfloat16)
-
-
 def share_kernel(
     count,
-    sums_ref,
-    assign_ref,
-    group_ref,
-    ctf_ref,
+    cap,
+    images_hbm,
+    assign_hbm,
+    turn_hbm,
+    group_hbm,
+    ctf_hbm,
     average_ref,
     lever_ref,
     partner_ref,
+    images_ref,
+    assign_ref,
+    turn_ref,
+    group_ref,
+    ctf_ref,
+    order_row,
+    order_ref,
+    slot_weights,
+    sums_ref,
+    own_sums,
     own_code,
     codes,
     landed,
     staged,
     gathered,
     average,
+    loads,
     code_send,
     code_recv,
     quad_send,
@@ -126,6 +119,18 @@
     layer = me // QUAD
     spot = me % QUAD
     particles = assign_ref.shape[1]
+    slots = count * cap
+
+    pairs = (
+        (assign_hbm, assign_ref),
+        (group_hbm, group_ref),
+        (ctf_hbm, ctf_ref),
+        (turn_hbm, turn_ref),
+        (images_hbm, images_ref),
+    )
+    moves = [pltpu.make_async_copy(a, b, loads.at[n]) for n, (a, b) in enumerate(pairs)]
+    for move in moves:
+        move.start()
 
     barrier = pltpu.get_barrier_semaphore()
 
@@ -141,7 +146,39 @@
 
     lax.fori_loop(1, count, greet, 0)
     lax.fori_loop(0, layers, greet_other, 0)
+    for move in moves[:3]:
+        move.wait()
     own_code[0] = jnp.concatenate([assign_ref[...], group_ref[...]], axis=1).astype(jnp.float32)
+    line = lax.broadcasted_iota(jnp.int32, (particles, particles), 0)
+    across = lax.broadcasted_iota(jnp.int32, (particles, particles), 1)
+
+    def as_column(row):
+        return jnp.sum(jnp.where(line == across, row, 0), axis=1, keepdims=True)
+
+    same = (as_column(assign_ref[...]) == assign_ref[...]) & (line < across)
+    rank = jnp.sum(jnp.where(same, 1, 0), axis=0, keepdims=True)
+    places = assign_ref[...] * cap + rank
+    taken = one_hot(places, slots)
+    filled = as_column(places) == lax.broadcasted_iota(jnp.int32, (particles, slots), 1)
+    numbers = lax.broadcasted_iota(jnp.int32, (particles, slots), 0)
+    order_row[...] = jnp.sum(jnp.where(filled, numbers, 0), axis=0, keepdims=True)
+
+    def to_slots(values):
+        return lax.dot_general(
+            values,
+            taken,
+            (((1,), (1,)), ((), ())),
+            precision=HIGHEST,
+            preferred_element_type=jnp.float32,
+        )
+
+    order_move = pltpu.make_async_copy(order_row, order_ref, loads.at[0])
+    order_move.start()
+    weights = columns_of(ctf_ref[...], group_ref[...])
+    slot_weights[...] = to_slots(weights)
+    order_move.wait()
+    for move in moves[3:]:
+        move.wait()
     pl.semaphore_wait(barrier, count - 1 + layers)
 
     def code_copy(source, peer):
@@ -198,17 +235,19 @@
         code_copy(me, lax.rem(me + k, count)).start()
         return 0
 
-    def send_quad(k, _):
-        level = lax.rem(layer + k, layers)
-        for j in range(1, QUAD):
-            quad_copy(level, spot, lax.rem(spot + j, QUAD)).start()
-        return 0
-
-    lax.fori_loop(1, layers + 1, send_quad, 0)
     lax.fori_loop(1, count, send_code, 0)
 
+    def class_sum(owner):
+        columns = pltpu.roll(slot_weights[...], lax.rem(slots - owner * cap, slots), 1)
+        total = jnp.zeros(images_ref.shape[1:], jnp.float32)
+        for place in range(cap):
+            particle = jnp.clip(order_ref[0, owner * cap + place], 0, images_ref.shape[0] - 1)
+            image = align(images_ref[particle], turn_ref[0, particle])
+            total += stacked(columns, place, image.shape[1]) * image
+        return total
+
     def quad_sum(level):
-        total = sums_ref[level * QUAD + spot].astype(jnp.float32)
+        total = own_sums[level]
         for j in range(1, QUAD):
             source = lax.rem(spot + j, QUAD)
             quad_copy(level, source, source).wait_recv()
@@ -221,7 +260,21 @@
         far_copy(layer, level).start()
         return 0
 
-    lax.fori_loop(1, layers, send_far, 0)
+    def sum_level(k, _):
+        level = lax.rem(layer + k, layers)
+        for j in range(1, QUAD):
+            target = lax.rem(spot + j, QUAD)
+            sums_ref[level * QUAD + target] = class_sum(level * QUAD + target).astype(jnp.bfloat16)
+            quad_copy(level, spot, target).start()
+        own_sums[level] = class_sum(level * QUAD + spot)
+
+        @pl.when(k > 1)
+        def _():
+            send_far(k - 1, 0)
+
+        return 0
+
+    lax.fori_loop(1, layers + 1, sum_level, 0)
 
     def tally(code):
         owners = one_hot(code[:, :particles].astype(jnp.int32), count)
@@ -265,7 +318,6 @@
 
     lax.fori_loop(0, layers, send_avg, 0)
     average_ref[...] = average[...]
-    weights = columns_of(table, group_ref[...])
     chosen = jnp.dot(
         den,
         one_hot(assign_ref[...], count),
@@ -308,18 +360,24 @@
 
 
 def compare_kernel(
+    assign_hbm,
+    turn_hbm,
+    group_hbm,
+    ctf_hbm,
+    partner_hbm,
+    average_hbm,
+    lever_hbm,
+    images_ref,
+    residual_ref,
+    scores_ref,
+    average_out,
+    lever_out,
     assign_ref,
     turn_ref,
     group_ref,
     ctf_ref,
     partner_ref,
-    average_ref,
-    lever_ref,
-    images_ref,
-    residual_ref,
-    scores_ref,
-    average_out,
-    lever_out,
+    loads,
     columns_ref,
     image_power,
     predicted_power,
@@ -329,9 +387,23 @@
 
     @pl.when(step == 0)
     def _():
+        pairs = (
+            (group_hbm, group_ref),
+            (ctf_hbm, ctf_ref),
+            (assign_hbm, assign_ref),
+            (turn_hbm, turn_ref),
+            (average_hbm, average_out),
+            (lever_hbm, lever_out),
+            (partner_hbm, partner_ref),
+        )
+        moves = [pltpu.make_async_copy(a, b, loads.at[n]) for n, (a, b) in enumerate(pairs)]
+        for move in moves:
+            move.start()
+        for move in moves[:2]:
+            move.wait()
         fill_columns(columns_ref, ctf_ref, group_ref)
-        average_out[...] = average_ref[...]
-        lever_out[...] = lever_ref[...]
+        for move in moves[2:]:
+            move.wait()
 
     columns = step_columns(columns_ref, step)
     rows, angles = images_ref.shape[1:]
@@ -347,7 +419,7 @@
         owner = assign_ref[0, particle]
         rounded = (weight * partner_ref[owner].astype(jnp.float32)).astype(jnp.bfloat16)
         predicted = rounded.astype(jnp.float32)
-        residual_ref[place] = (align(image, turn_ref[0, particle]) - predicted).astype(jnp.bfloat16)
+        residual_ref[place] = (align(raw_image, turn_ref[0, particle]) - predicted).astype(jnp.bfloat16)
         cross = lax.dot_general(
             raw_image, rounded, (((0,), (0,)), ((), ())), preferred_element_type=jnp.float32
         )
@@ -403,33 +475,31 @@
     count = lax.axis_size("cls")
     layers = count // QUAD
     steps = number // STEP
-    params = pltpu.CompilerParams(vmem_limit_bytes=VMEM_BYTES)
+    cap = max(2, 2 * number // count)
+    slots = count * cap
+    params = pltpu.CompilerParams(vmem_limit_bytes=WIDE_BYTES)
     block = pl.BlockSpec((STEP, rows, angles), lambda i: (i, 0, 0))
 
-    sums = pl.pallas_call(
-        sums_kernel,
-        grid=(steps,),
-        out_shape=jax.ShapeDtypeStruct((count, rows, angles), jnp.bfloat16),
-        in_specs=[smem(), smem(), vmem(), vmem(), block],
-        out_specs=vmem(),
-        scratch_shapes=[
-            pltpu.VMEM((count, rows, angles), jnp.float32),
-            pltpu.VMEM((shells, 128), jnp.float32),
-        ],
-        compiler_params=pltpu.CompilerParams(vmem_limit_bytes=WIDE_BYTES),
-        name="class_sums",
-    )(assign, rotation, group, table, images)
-
     average, lever, partner = pl.pallas_call(
-        functools.partial(share_kernel, count),
+        functools.partial(share_kernel, count, cap),
         out_shape=(
             jax.ShapeDtypeStruct((rows, angles), jnp.bfloat16),
             jax.ShapeDtypeStruct((1, number), jnp.bfloat16),
             jax.ShapeDtypeStruct((count, rows, angles), jnp.bfloat16),
         ),
-        in_specs=[vmem(), vmem(), vmem(), vmem()],
+        in_specs=[anywhere()] * 5,
         out_specs=(vmem(), vmem(), pl.BlockSpec(memory_space=pl.ANY)),
         scratch_shapes=[
+            pltpu.VMEM((number, rows, angles), jnp.bfloat16),
+            pltpu.VMEM((1, number), jnp.int32),
+            pltpu.SMEM((1, number), jnp.int32),
+            pltpu.VMEM((1, number), jnp.int32),
+            pltpu.VMEM(table.shape, jnp.float32),
+            pltpu.VMEM((1, slots), jnp.int32),
+            pltpu.SMEM((1, slots), jnp.int32),
+            pltpu.VMEM((shells, slots), jnp.float32),
+            pltpu.VMEM((count, rows, angles), jnp.bfloat16),
+            pltpu.VMEM((layers, rows, angles), jnp.float32),
             pltpu.VMEM((1, 1, 2 * number), jnp.float32),
             pltpu.VMEM((count, 1, 2 * number), jnp.float32),
             pltpu.VMEM((count, rows, angles), jnp.bfloat16),
@@ -437,14 +507,15 @@
             pltpu.VMEM((layers, rows, angles), jnp.bfloat16),
             pltpu.VMEM((rows, angles), jnp.bfloat16),
         ]
+        + [pltpu.SemaphoreType.DMA((5,))]
         + [pltpu.SemaphoreType.DMA((count,))] * 4
         + [pltpu.SemaphoreType.DMA((layers,))] * 3
         + [pltpu.SemaphoreType.DMA((count,))] * 2,
         compiler_params=pltpu.CompilerParams(
-            collective_id=0, has_side_effects=True, vmem_limit_bytes=VMEM_BYTES
+            collective_id=0, has_side_effects=True, vmem_limit_bytes=WIDE_BYTES
         ),
         name="share",
-    )(sums, assign, group, table)
+    )(images, assign, rotation, group, table)
 
     residual, scores, average, lever = pl.pallas_call(
         compare_kernel,
@@ -455,9 +526,17 @@
             jax.ShapeDtypeStruct((rows, angles), jnp.bfloat16),
             jax.ShapeDtypeStruct((1, number), jnp.bfloat16),
         ),
-        in_specs=[smem(), smem()] + [vmem()] * 5 + [block],
+        in_specs=[anywhere()] * 7 + [block],
         out_specs=(block, vmem(), vmem(), vmem()),
-        scratch_shapes=[pltpu.VMEM((shells, 128), jnp.float32)]
+        scratch_shapes=[
+            pltpu.SMEM((1, number), jnp.int32),
+            pltpu.SMEM((1, number), jnp.int32),
+            pltpu.VMEM((1, number), jnp.int32),
+            pltpu.VMEM(table.shape, jnp.float32),
+            pltpu.VMEM((count, rows, angles), jnp.bfloat16),
+            pltpu.SemaphoreType.DMA((7,)),
+            pltpu.VMEM((shells, 128), jnp.float32),
+        ]
         + [pltpu.VMEM((number * 8, angles), jnp.float32)] * 3,
         compiler_params=params,
         name="compare",

time: 50.2 us -> 46.5 us (0.926)
  local copies, waits for them, and re-layouts: 2.64 us -> 0 us
  Pallas kernels: 46.5 us -> 45.6 us
    unnamed x12 -> x0, local copies, waits for them, and re-layouts: 2.64 us -> none
    pallas_call x2 -> x1, Pallas kernels: 35 us -> 32.8 us  [body(): pl.pallas_call(functools.partial(share_kernel, count, cap), out_shape=(ja...]
    pallas_call x1, Pallas kernels: 11.5 us -> 12.8 us  [body(): pl.pallas_call(compare_kernel, grid=(steps,), out_shape=(jax.ShapeDtypeSt...]
where the time goes in v1:
time: 46.5 us; the launch traced here: 46.3 us
  Pallas kernels  45.6 us (98%)
  between operations  0.64 us (1%)
    pallas_call x1, Pallas kernels, body(): pl.pallas_call(functools.partial(share_kernel, count, cap), out_shape=(ja...  32.8 us
    pallas_call x1, Pallas kernels, body(): pl.pallas_call(compare_kernel, grid=(steps,), out_shape=(jax.ShapeDtypeSt...  12.8 us

profile of v1, /device:TPU:0, one launch (start us, length us, event | category | flops | bytes accessed | tf_op | source)
XLA Modules:
  0.0 46.3 jit_solution(10697248513188389675)
XLA Ops:
  0.6 32.8 %share.1 = (bf16[128,128]{1,0:T(8,128)(2,1)}, bf16[1,64]{1,0:T(2,128)(2,1)}, bf16[16,128,128]{2,1,0:T(8,128)(2,1)}) custom-call(bf16[64,128,128]{2,1,0:T(8,128)(2,1)} %bitcast.7, s32[1,64]{1,0:T(1,128)} %assign_hbm.3, s32[1,64]{1,0:T(1,128)} %turn_hbm.3, s32[1,64]{1,0:T(1,128)} %group_hbm.3, f32[64,256]{1,0:T(8,128)} %bitcast.9), custom_call_target="tpu_custom_call" | custom-call | tf_op jit(solution)/shard_map/share/pallas_call | solution.py:483
  33.5 12.8 %compare.1 = (bf16[64,128,128]{2,1,0:T(8,128)(2,1)}, bf16[36,64]{1,0:T(8,128)(2,1)}, bf16[128,128]{1,0:T(8,128)(2,1)}, bf16[1,64]{1,0:T(2,128)(2,1)}) custom-call(s32[1,64]{1,0:T(1,128)} %assign_hbm.3, s32[1,64]{1,0:T(1,128)} %turn_hbm.3, s32[1,64]{1,0:T(1,128)} %group_hbm.3, f32[64,256]{1,0:T(8,128)} %bitcast.10, ...), custom_call_target="tpu_custom_call" | custom-call | tf_op jit(solution)/shard_map/compare/pallas_call | solution.py:520

commit v2 on v1

--- a/solution.py
+++ b/solution.py
@@ -3,6 +3,7 @@
 
 import jax
 import jax.numpy as jnp
+import numpy as np
 from jax import lax
 from jax.experimental import pallas as pl
 from jax.experimental.pallas import tpu as pltpu
@@ -34,13 +35,20 @@
     return offset, first, second
 
 
-def align(image, turn):
-    angles = image.shape[1]
-    offset, first, second = mix(turn, angles)
-    rolled = pltpu.roll(image, offset, 1)
-    return first * rolled.astype(jnp.float32) + second * pltpu.roll(rolled, 1, 1).astype(
-        jnp.float32
-    )
+def rotation_table(angles):
+    turns = np.arange(NROT)
+    offset = turns * angles // NROT
+    fraction = (turns * angles % NROT).astype(np.float32) / np.float32(NROT)
+    table = np.zeros((NROT, angles, angles), np.float32)
+    source = np.arange(angles)
+    for r in range(NROT):
+        table[r, source, (source + offset[r]) % angles] = np.float32(1.0) - fraction[r]
+        table[r, source, (source + offset[r] + 1) % angles] = fraction[r]
+    return jnp.asarray(table.astype(jnp.bfloat16))
+
+
+def align(image, rotation):
+    return jnp.dot(image, rotation, preferred_element_type=jnp.float32)
 
 
 def one_hot(row, size):
@@ -82,6 +90,7 @@
     turn_hbm,
     group_hbm,
     ctf_hbm,
+    table_hbm,
     average_ref,
     lever_ref,
     partner_ref,
@@ -90,6 +99,7 @@
     turn_ref,
     group_ref,
     ctf_ref,
+    table_ref,
     order_row,
     order_ref,
     slot_weights,
@@ -127,6 +137,7 @@
         (ctf_hbm, ctf_ref),
         (turn_hbm, turn_ref),
         (images_hbm, images_ref),
+        (table_hbm, table_ref),
     )
     moves = [pltpu.make_async_copy(a, b, loads.at[n]) for n, (a, b) in enumerate(pairs)]
     for move in moves:
@@ -242,7 +253,7 @@
         total = jnp.zeros(images_ref.shape[1:], jnp.float32)
         for place in range(cap):
             particle = jnp.clip(order_ref[0, owner * cap + place], 0, images_ref.shape[0] - 1)
-            image = align(images_ref[particle], turn_ref[0, particle])
+            image = align(images_ref[particle], table_ref[turn_ref[0, particle]])
             total += stacked(columns, place, image.shape[1]) * image
         return total
 
@@ -288,10 +299,15 @@
 
     def add_code(k, counts):
         source = lax.rem(me + count - k, count)
+        return counts + tally(codes[source])
+
+    def wait_code(k, _):
+        source = lax.rem(me + count - k, count)
         code_copy(source, source).wait_recv()
-        return counts + tally(codes[source])
-
-    counts = lax.fori_loop(1, count, add_code, tally(own_code[0]))
+        return 0
+
+    lax.fori_loop(1, count, wait_code, 0)
+    counts = lax.fori_loop(1, count, add_code, tally(own_code[0]), unroll=min(count - 1, 15))
     table = ctf_ref[...]
     den = lax.dot_general(
         table * table,
@@ -367,6 +383,7 @@
     partner_hbm,
     average_hbm,
     lever_hbm,
+    table_hbm,
     images_ref,
     residual_ref,
     scores_ref,
@@ -377,6 +394,7 @@
     group_ref,
     ctf_ref,
     partner_ref,
+    table_ref,
     loads,
     columns_ref,
     image_power,
@@ -395,6 +413,7 @@
             (average_hbm, average_out),
             (lever_hbm, lever_out),
             (partner_hbm, partner_ref),
+            (table_hbm, table_ref),
         )
         moves = [pltpu.make_async_copy(a, b, loads.at[n]) for n, (a, b) in enumerate(pairs)]
         for move in moves:
@@ -419,7 +438,7 @@
         owner = assign_ref[0, particle]
         rounded = (weight * partner_ref[owner].astype(jnp.float32)).astype(jnp.bfloat16)
         predicted = rounded.astype(jnp.float32)
-        residual_ref[place] = (align(raw_image, turn_ref[0, particle]) - predicted).astype(jnp.bfloat16)
+        residual_ref[place] = (align(raw_image, table_ref[turn_ref[0, particle]]) - predicted).astype(jnp.bfloat16)
         cross = lax.dot_general(
             raw_image, rounded, (((0,), (0,)), ((), ())), preferred_element_type=jnp.float32
         )
@@ -471,6 +490,7 @@
     images = particles[0]
     number, rows, angles = images.shape
     table = ctf.T
+    rotations = rotation_table(angles)
     shells = ctf.shape[1]
     count = lax.axis_size("cls")
     layers = count // QUAD
@@ -487,7 +507,7 @@
             jax.ShapeDtypeStruct((1, number), jnp.bfloat16),
             jax.ShapeDtypeStruct((count, rows, angles), jnp.bfloat16),
         ),
-        in_specs=[anywhere()] * 5,
+        in_specs=[anywhere()] * 6,
         out_specs=(vmem(), vmem(), pl.BlockSpec(memory_space=pl.ANY)),
         scratch_shapes=[
             pltpu.VMEM((number, rows, angles), jnp.bfloat16),
@@ -495,6 +515,7 @@
             pltpu.SMEM((1, number), jnp.int32),
             pltpu.VMEM((1, number), jnp.int32),
             pltpu.VMEM(table.shape, jnp.float32),
+            pltpu.VMEM(rotations.shape, jnp.bfloat16),
             pltpu.VMEM((1, slots), jnp.int32),
             pltpu.SMEM((1, slots), jnp.int32),
             pltpu.VMEM((shells, slots), jnp.float32),
@@ -507,7 +528,7 @@
             pltpu.VMEM((layers, rows, angles), jnp.bfloat16),
             pltpu.VMEM((rows, angles), jnp.bfloat16),
         ]
-        + [pltpu.SemaphoreType.DMA((5,))]
+        + [pltpu.SemaphoreType.DMA((6,))]
         + [pltpu.SemaphoreType.DMA((count,))] * 4
         + [pltpu.SemaphoreType.DMA((layers,))] * 3
         + [pltpu.SemaphoreType.DMA((count,))] * 2,
@@ -515,7 +536,7 @@
             collective_id=0, has_side_effects=True, vmem_limit_bytes=WIDE_BYTES
         ),
         name="share",
-    )(images, assign, rotation, group, table)
+    )(images, assign, rotation, group, table, rotations)
 
     residual, scores, average, lever = pl.pallas_call(
         compare_kernel,
@@ -526,7 +547,7 @@
             jax.ShapeDtypeStruct((rows, angles), jnp.bfloat16),
             jax.ShapeDtypeStruct((1, number), jnp.bfloat16),
         ),
-        in_specs=[anywhere()] * 7 + [block],
+        in_specs=[anywhere()] * 8 + [block],
         out_specs=(block, vmem(), vmem(), vmem()),
         scratch_shapes=[
             pltpu.SMEM((1, number), jnp.int32),
@@ -534,13 +555,14 @@
             pltpu.VMEM((1, number), jnp.int32),
             pltpu.VMEM(table.shape, jnp.float32),
             pltpu.VMEM((count, rows, angles), jnp.bfloat16),
-            pltpu.SemaphoreType.DMA((7,)),
+            pltpu.VMEM(rotations.shape, jnp.bfloat16),
+            pltpu.SemaphoreType.DMA((8,)),
             pltpu.VMEM((shells, 128), jnp.float32),
         ]
         + [pltpu.VMEM((number * 8, angles), jnp.float32)] * 3,
         compiler_params=params,
         name="compare",
-    )(assign, rotation, group, table, partner, average, lever, images)
+    )(assign, rotation, group, table, partner, average, lever, rotations, images)
     return (average[None, None], residual[None], scores.T[None], lever)
 
 

time: 46.5 us -> 38.7 us (0.83)
  Pallas kernels: 45.6 us -> 37.6 us
    pallas_call x1, Pallas kernels: 32.8 us -> 28 us  [body(): pl.pallas_call(functools.partial(share_kernel, count, cap), out_shape=(ja...]
    pallas_call x1, Pallas kernels: 12.8 us -> 9.6 us  [body(): pl.pallas_call(compare_kernel, grid=(steps,), out_shape=(jax.ShapeDtypeSt...]
where the time goes in v2:
time: 38.7 us; the launch traced here: 38.2 us
  Pallas kernels  37.6 us (97%)
  between operations  0.64 us (2%)
    pallas_call x1, Pallas kernels, body(): pl.pallas_call(functools.partial(share_kernel, count, cap), out_shape=(ja...  28 us
    pallas_call x1, Pallas kernels, body(): pl.pallas_call(compare_kernel, grid=(steps,), out_shape=(jax.ShapeDtypeSt...  9.6 us

profile of v2, /device:TPU:0, one launch (start us, length us, event | category | flops | bytes accessed | tf_op | source)
XLA Modules:
  0.0 38.2 jit_solution(17446095388993067258)
XLA Ops:
  0.6 28.0 %share.1 = (bf16[128,128]{1,0:T(8,128)(2,1)}, bf16[1,64]{1,0:T(2,128)(2,1)}, bf16[16,128,128]{2,1,0:T(8,128)(2,1)}) custom-call(bf16[64,128,128]{2,1,0:T(8,128)(2,1)} %bitcast.7, s32[1,64]{1,0:T(1,128)} %assign_hbm.3, s32[1,64]{1,0:T(1,128)} %turn_hbm.3, s32[1,64]{1,0:T(1,128)} %group_hbm.3, f32[64,256]{1,0:T(8,128)} %bitcast.9, ...), custom_call_target="tpu_custom_call" | custom-call | tf_op jit(solution)/shard_map/share/pallas_call | solution.py:503
  28.6 9.6 %compare.1 = (bf16[64,128,128]{2,1,0:T(8,128)(2,1)}, bf16[36,64]{1,0:T(8,128)(2,1)}, bf16[128,128]{1,0:T(8,128)(2,1)}, bf16[1,64]{1,0:T(2,128)(2,1)}) custom-call(s32[1,64]{1,0:T(1,128)} %assign_hbm.3, s32[1,64]{1,0:T(1,128)} %turn_hbm.3, s32[1,64]{1,0:T(1,128)} %group_hbm.3, f32[64,256]{1,0:T(8,128)} %bitcast.10, ...), custom_call_target="tpu_custom_call" | custom-call | tf_op jit(solution)/shard_map/compare/pallas_call | solution.py:541

commit v3 on v2

--- a/solution.py
+++ b/solution.py
@@ -12,6 +12,7 @@
 NROT = 36
 TAU = 1.0
 STEP = 8
+BATCH = 4
 QUAD = 4
 MESH = pl.DeviceIdType.MESH
 HIGHEST = lax.Precision.HIGHEST
@@ -273,11 +274,15 @@
 
     def sum_level(k, _):
         level = lax.rem(layer + k, layers)
-        for j in range(1, QUAD):
-            target = lax.rem(spot + j, QUAD)
-            sums_ref[level * QUAD + target] = class_sum(level * QUAD + target).astype(jnp.bfloat16)
-            quad_copy(level, spot, target).start()
-        own_sums[level] = class_sum(level * QUAD + spot)
+        for pair in range(1, QUAD, 2):
+            targets = [lax.rem(spot + j, QUAD) for j in (pair, pair + 1)]
+            totals = [class_sum(level * QUAD + target) for target in targets]
+            for j, target, total in zip((pair, pair + 1), targets, totals):
+                if j < QUAD:
+                    sums_ref[level * QUAD + target] = total.astype(jnp.bfloat16)
+                    quad_copy(level, spot, target).start()
+                else:
+                    own_sums[level] = total
 
         @pl.when(k > 1)
         def _():
@@ -430,7 +435,7 @@
     def fold(values):
         return jnp.sum(values.reshape(rows // 8, 8, angles), axis=0)
 
-    for place in range(STEP):
+    def work(place):
         particle = step * STEP + place
         raw_image = images_ref[place]
         image = raw_image.astype(jnp.float32)
@@ -438,17 +443,25 @@
         owner = assign_ref[0, particle]
         rounded = (weight * partner_ref[owner].astype(jnp.float32)).astype(jnp.bfloat16)
         predicted = rounded.astype(jnp.float32)
-        residual_ref[place] = (align(raw_image, table_ref[turn_ref[0, particle]]) - predicted).astype(jnp.bfloat16)
+        aligned = align(raw_image, table_ref[turn_ref[0, particle]])
+        residual = (aligned - predicted).astype(jnp.bfloat16)
         cross = lax.dot_general(
             raw_image, rounded, (((0,), (0,)), ((), ())), preferred_element_type=jnp.float32
         )
         turned = cross[:8]
         for tile in range(1, angles // 8):
             turned += pltpu.roll(cross[tile * 8 : tile * 8 + 8], angles - tile * 8, 1)
-        spot = pl.ds(pl.multiple_of(particle * 8, 8), 8)
-        folded[spot, :] = turned
-        image_power[spot, :] = fold(image * image)
-        predicted_power[spot, :] = fold(predicted * predicted)
+        return residual, turned, fold(image * image), fold(predicted * predicted)
+
+    for start in range(0, STEP, BATCH):
+        places = range(start, start + BATCH)
+        results = [work(place) for place in places]
+        for place, (residual, turned, first, second) in zip(places, results):
+            spot = pl.ds(pl.multiple_of((step * STEP + place) * 8, 8), 8)
+            residual_ref[place] = residual
+            folded[spot, :] = turned
+            image_power[spot, :] = first
+            predicted_power[spot, :] = second
 
     @pl.when(step == pl.num_programs(0) - 1)
     def _():

time: 38.7 us -> 38.4 us (level)
  no operation moved by 1% of the time
where the time goes in v3:
time: 38.4 us; the launch traced here: 38.1 us
  Pallas kernels  37.4 us (97%)
  between operations  0.64 us (2%)
    pallas_call x1, Pallas kernels, body(): pl.pallas_call(functools.partial(share_kernel, count, cap), out_shape=(ja...  27.8 us
    pallas_call x1, Pallas kernels, body(): pl.pallas_call(compare_kernel, grid=(steps,), out_shape=(jax.ShapeDtypeSt...  9.6 us

profile of v3, /device:TPU:0, one launch (start us, length us, event | category | flops | bytes accessed | tf_op | source)
XLA Modules:
  0.0 38.1 jit_solution(13436216275570612058)
XLA Ops:
  0.6 27.8 %share.1 = (bf16[128,128]{1,0:T(8,128)(2,1)}, bf16[1,64]{1,0:T(2,128)(2,1)}, bf16[16,128,128]{2,1,0:T(8,128)(2,1)}) custom-call(bf16[64,128,128]{2,1,0:T(8,128)(2,1)} %bitcast.7, s32[1,64]{1,0:T(1,128)} %assign_hbm.3, s32[1,64]{1,0:T(1,128)} %turn_hbm.3, s32[1,64]{1,0:T(1,128)} %group_hbm.3, f32[64,256]{1,0:T(8,128)} %bitcast.9, ...), custom_call_target="tpu_custom_call" | custom-call | tf_op jit(solution)/shard_map/share/pallas_call | solution.py:516
  28.5 9.6 %compare.1 = (bf16[64,128,128]{2,1,0:T(8,128)(2,1)}, bf16[36,64]{1,0:T(8,128)(2,1)}, bf16[128,128]{1,0:T(8,128)(2,1)}, bf16[1,64]{1,0:T(2,128)(2,1)}) custom-call(s32[1,64]{1,0:T(1,128)} %assign_hbm.3, s32[1,64]{1,0:T(1,128)} %turn_hbm.3, s32[1,64]{1,0:T(1,128)} %group_hbm.3, f32[64,256]{1,0:T(8,128)} %bitcast.10, ...), custom_call_target="tpu_custom_call" | custom-call | tf_op jit(solution)/shard_map/compare/pallas_call | solution.py:554

commit v4 on v3

--- a/solution.py
+++ b/solution.py
@@ -13,6 +13,7 @@
 TAU = 1.0
 STEP = 8
 BATCH = 4
+CHUNK = 16
 QUAD = 4
 MESH = pl.DeviceIdType.MESH
 HIGHEST = lax.Precision.HIGHEST
@@ -95,7 +96,10 @@
     average_ref,
     lever_ref,
     partner_ref,
+    turned_hbm,
     images_ref,
+    turned_ref,
+    leave,
     assign_ref,
     turn_ref,
     group_ref,
@@ -243,11 +247,6 @@
             device_id_type=MESH,
         )
 
-    def send_code(k, _):
-        code_copy(me, lax.rem(me + k, count)).start()
-        return 0
-
-    lax.fori_loop(1, count, send_code, 0)
 
     def class_sum(owner):
         columns = pltpu.roll(slot_weights[...], lax.rem(slots - owner * cap, slots), 1)
@@ -283,6 +282,13 @@
                     quad_copy(level, spot, target).start()
                 else:
                     own_sums[level] = total
+
+        for j in range(1, QUAD):
+            code_copy(me, level * QUAD + lax.rem(spot + j, QUAD)).start()
+
+        @pl.when(k < layers)
+        def _():
+            code_copy(me, level * QUAD + spot).start()
 
         @pl.when(k > 1)
         def _():
@@ -357,6 +363,19 @@
 
     lax.fori_loop(0, layers, pass_on, 0)
 
+    def turned_move(chunk):
+        piece = pl.ds(chunk * CHUNK, CHUNK)
+        return pltpu.make_async_copy(turned_ref.at[piece], turned_hbm.at[piece], leave.at[chunk])
+
+    def turn_chunk(chunk, _):
+        for n in range(CHUNK):
+            turned_ref[chunk * CHUNK + n] = images_ref[chunk * CHUNK + n].T
+        turned_move(chunk).start()
+        return 0
+
+    chunks = particles // CHUNK
+    lax.fori_loop(0, chunks, turn_chunk, 0)
+
     def finish_code(k, _):
         code_copy(me, lax.rem(me + k, count)).wait_send()
         return 0
@@ -378,6 +397,8 @@
     lax.fori_loop(1, count, finish_code, 0)
     lax.fori_loop(1, layers, finish_far, 0)
     lax.fori_loop(0, layers, finish_level, 0)
+    for chunk in range(chunks):
+        turned_move(chunk).wait()
 
 
 def compare_kernel(
@@ -390,6 +411,7 @@
     lever_hbm,
     table_hbm,
     images_ref,
+    turned_ref,
     residual_ref,
     scores_ref,
     average_out,
@@ -445,9 +467,7 @@
         predicted = rounded.astype(jnp.float32)
         aligned = align(raw_image, table_ref[turn_ref[0, particle]])
         residual = (aligned - predicted).astype(jnp.bfloat16)
-        cross = lax.dot_general(
-            raw_image, rounded, (((0,), (0,)), ((), ())), preferred_element_type=jnp.float32
-        )
+        cross = jnp.dot(turned_ref[place], rounded, preferred_element_type=jnp.float32)
         turned = cross[:8]
         for tile in range(1, angles // 8):
             turned += pltpu.roll(cross[tile * 8 : tile * 8 + 8], angles - tile * 8, 1)
@@ -512,18 +532,22 @@
     slots = count * cap
     params = pltpu.CompilerParams(vmem_limit_bytes=WIDE_BYTES)
     block = pl.BlockSpec((STEP, rows, angles), lambda i: (i, 0, 0))
-
-    average, lever, partner = pl.pallas_call(
+    flipped = pl.BlockSpec((STEP, angles, rows), lambda i: (i, 0, 0))
+
+    average, lever, partner, turned = pl.pallas_call(
         functools.partial(share_kernel, count, cap),
         out_shape=(
             jax.ShapeDtypeStruct((rows, angles), jnp.bfloat16),
             jax.ShapeDtypeStruct((1, number), jnp.bfloat16),
             jax.ShapeDtypeStruct((count, rows, angles), jnp.bfloat16),
+            jax.ShapeDtypeStruct((number, angles, rows), jnp.bfloat16),
         ),
         in_specs=[anywhere()] * 6,
-        out_specs=(vmem(), vmem(), pl.BlockSpec(memory_space=pl.ANY)),
+        out_specs=(vmem(), vmem(), anywhere(), anywhere()),
         scratch_shapes=[
             pltpu.VMEM((number, rows, angles), jnp.bfloat16),
+            pltpu.VMEM((number, angles, rows), jnp.bfloat16),
+            pltpu.SemaphoreType.DMA((number // CHUNK,)),
             pltpu.VMEM((1, number), jnp.int32),
             pltpu.SMEM((1, number), jnp.int32),
             pltpu.VMEM((1, number), jnp.int32),
@@ -560,7 +584,7 @@
             jax.ShapeDtypeStruct((rows, angles), jnp.bfloat16),
             jax.ShapeDtypeStruct((1, number), jnp.bfloat16),
         ),
-        in_specs=[anywhere()] * 8 + [block],
+        in_specs=[anywhere()] * 8 + [block, flipped],
         out_specs=(block, vmem(), vmem(), vmem()),
         scratch_shapes=[
             pltpu.SMEM((1, number), jnp.int32),
@@ -575,7 +599,7 @@
         + [pltpu.VMEM((number * 8, angles), jnp.float32)] * 3,
         compiler_params=params,
         name="compare",
-    )(assign, rotation, group, table, partner, average, lever, rotations, images)
+    )(assign, rotation, group, table, partner, average, lever, rotations, images, turned)
     return (average[None, None], residual[None], scores.T[None], lever)
 
 

time: 38.4 us -> 39.3 us (1.023)
  Pallas kernels: 37.4 us -> 38.3 us
    pallas_call x1, Pallas kernels: 27.8 us -> 28.5 us  [body(): pl.pallas_call(functools.partial(share_kernel, count, cap), out_shape=(ja...]
where the time goes in v4:
time: 39.3 us; the launch traced here: 39 us
  Pallas kernels  38.3 us (97%)
  between operations  0.64 us (2%)
    pallas_call x1, Pallas kernels, body(): pl.pallas_call(functools.partial(share_kernel, count, cap), out_shape=(ja...  28.5 us
    pallas_call x1, Pallas kernels, body(): pl.pallas_call(compare_kernel, grid=(steps,), out_shape=(jax.ShapeDtypeSt...  9.85 us

profile of v4, /device:TPU:0, one launch (start us, length us, event | category | flops | bytes accessed | tf_op | source)
XLA Modules:
  0.0 39.0 jit_solution(5829794153541183431)
XLA Ops:
  0.6 28.5 %share.1 = (bf16[128,128]{1,0:T(8,128)(2,1)}, bf16[1,64]{1,0:T(2,128)(2,1)}, bf16[16,128,128]{2,1,0:T(8,128)(2,1)}, bf16[64,128,128]{2,1,0:T(8,128)(2,1)}) custom-call(bf16[64,128,128]{2,1,0:T(8,128)(2,1)} %bitcast.7, s32[1,64]{1,0:T(1,128)} %assign_hbm.3, s32[1,64]{1,0:T(1,128)} %turn_hbm.3, s32[1,64]{1,0:T(1,128)} %group_hbm.3, f32[64,256]{1,0:T(8,128)} %bitcast.9, ...), custom_call_target="tpu_custom_call" | custom-call | tf_op jit(solution)/shard_map/share/pallas_call | solution.py:537
  29.1 9.9 %compare.1 = (bf16[64,128,128]{2,1,0:T(8,128)(2,1)}, bf16[36,64]{1,0:T(8,128)(2,1)}, bf16[128,128]{1,0:T(8,128)(2,1)}, bf16[1,64]{1,0:T(2,128)(2,1)}) custom-call(s32[1,64]{1,0:T(1,128)} %assign_hbm.3, s32[1,64]{1,0:T(1,128)} %turn_hbm.3, s32[1,64]{1,0:T(1,128)} %group_hbm.3, f32[64,256]{1,0:T(8,128)} %bitcast.10, ...), custom_call_target="tpu_custom_call" | custom-call | tf_op jit(solution)/shard_map/compare/pallas_call | solution.py:578
